TPU v7x, 32 devices: a whole 2x2x4 slice. The times are simulated.
32 devices in a mesh: blk: 2 (over y), grp: 16 (over z, x, core).
Axes of the slice: x: 2, y: 2, z: 4, core: 2. Of those that a mesh axis runs over, the one named last changes fastest.
Arguments:
- positions: float32 [3, 8192], P(None, ('blk', 'grp')), may hold values from -6 to 6
- velocities: float32 [3, 8192], P(None, ('blk', 'grp')), may hold values from -6 to 6
- accelerations: float32 [3, 8192], P(None, ('blk', 'grp')), may hold values from -4 to 4
- jerks: float32 [3, 8192], P(None, ('blk', 'grp')), may hold values from -4 to 4
- mass_weight: float32 [8192], P(('blk', 'grp')), may hold values from 0.3 to 3
- levels: int32 [8192], P(('blk', 'grp')), may hold values from 0 to 3, as said below
- active: int32 [2, 768], P(None, ('blk', 'grp')), may hold values from 0 to 255, as said below
- counts: int32 [2, 32], P(None, ('blk', 'grp')), may hold values from 1 to 24
Outputs:
- positions_out: float32 [3, 8192], P(None, ('blk', 'grp'))
- velocities_out: float32 [3, 8192], P(None, ('blk', 'grp'))
- accelerations_out: float32 [3, 8192], P(None, ('blk', 'grp'))
- jerks_out: float32 [3, 8192], P(None, ('blk', 'grp'))
- fresh_forces: float32 [2, 6, 768], P(None, None, ('blk', 'grp'))
Inputs may be any that keep to these rules, and one draw needn't show every extreme that they name: `active`: entries are local indices of the owner's particles; the live slots of one owner's list are distinct, dead slots hold 0. `levels`: particles not named in any list have level 2 or 3.
All inputs are finite; a program needn't handle non-finite values.
Results may differ from a plain program's by a relative error of at most 0.0003.
Values sent between devices are 32-bit elements; how exact they have to be, the bound alone decides.
A program may use at most 64 MiB of HBM per device.

v0:
```python
import jax
import jax.numpy as jnp
from jax import lax
from jax.sharding import PartitionSpec as P

STEP_BASE = 0.125
SOFTEN = 0.01


def passed_along(value, axis, steps):
    count = lax.axis_size(axis)
    pairs = [(source, (source + steps) % count) for source in range(count)]
    return lax.ppermute(value, axis, pairs)


def predict(pos, vel, acc, jerk, elapsed):
    pred_pos = pos + elapsed * (vel + elapsed * (acc * 0.5 + elapsed * jerk / 6.0))
    pred_vel = vel + elapsed * (acc + elapsed * jerk * 0.5)
    return (pred_pos, pred_vel)


def correct(pos, vel, acc, jerk, new_acc, new_jerk, stride, hit):
    half = 0.5 * stride
    square = stride * stride / 12.0
    vel_new = vel + half * (acc + new_acc) + square * (jerk - new_jerk)
    pos_new = pos + half * (vel + vel_new) + square * (acc - new_acc)
    return (
        jnp.where(hit, pos_new, pos),
        jnp.where(hit, vel_new, vel),
        jnp.where(hit, new_acc, acc),
        jnp.where(hit, new_jerk, jerk),
    )


def block_terms(iblock, jpart):
    dpos = jpart[0:3, :, None] - iblock[0:3, None, :]
    dvel = jpart[3:6, :, None] - iblock[3:6, None, :]
    dist = dpos[0] * dpos[0] + dpos[1] * dpos[1] + dpos[2] * dpos[2] + SOFTEN
    inverse = lax.rsqrt(dist)
    weight = jpart[6][:, None] * inverse * inverse * inverse
    radial = 3.0 * (dpos[0] * dvel[0] + dpos[1] * dvel[1] + dpos[2] * dvel[2]) * inverse * inverse
    accel = jnp.sum(weight[None] * dpos, axis=1)
    jerk = jnp.sum(weight[None] * (dvel - radial[None] * dpos), axis=1)
    return jnp.concatenate([accel, jerk], axis=0)


def pair_terms(ipart, jpart):
    rows = ipart.shape[1]
    width = 512 if rows % 512 == 0 else rows
    if width == rows:
        return block_terms(ipart, jpart)
    blocks = ipart.reshape(6, rows // width, width).transpose(1, 0, 2)
    result = lax.map(lambda iblock: block_terms(iblock, jpart), blocks)
    return result.transpose(1, 0, 2).reshape(6, rows)


def body(positions, velocities, accelerations, jerks, mass_weight, levels, active, counts):
    count_part = positions.shape[1]
    loop_len = lax.axis_size("blk")
    total_part = count_part * loop_len * lax.axis_size("grp")
    mass = mass_weight / total_part
    clock = jnp.zeros((count_part,), jnp.float32)
    stride = STEP_BASE * jnp.left_shift(jnp.ones_like(levels), levels).astype(jnp.float32)
    particle = jnp.arange(count_part, dtype=jnp.int32)
    slot = jnp.arange(active.shape[1], dtype=jnp.int32)
    pos, vel, acc, jerk = (positions, velocities, accelerations, jerks)
    recorded = []
    for step in range(2):
        now = STEP_BASE * (step + 1)
        elapsed = now - clock
        pred_pos, pred_vel = predict(pos, vel, acc, jerk, elapsed)
        live = slot < counts[step, 0]
        picker = ((active[step][:, None] == particle[None, :]) & live[:, None]).astype(jnp.float32)
        pred_both = jnp.concatenate([pred_pos, pred_vel], axis=0)
        chosen = jnp.dot(pred_both, picker.T, precision=lax.Precision.HIGHEST)
        jdata = jnp.concatenate([pred_pos, pred_vel, mass[None, :]], axis=0)
        row_actives = lax.all_gather(chosen, "grp", axis=1, tiled=True)
        travel = jdata
        partial_value = pair_terms(row_actives, travel)
        for turn in range(loop_len - 1):
            travel = passed_along(travel, "blk", 1)
            partial_value = partial_value + pair_terms(row_actives, travel)
        fresh = lax.psum_scatter(partial_value, "grp", scatter_dimension=1, tiled=True)
        recorded.append(jnp.where(live[None, :], fresh, jnp.zeros_like(fresh)))
        spread = jnp.dot(fresh, picker, precision=lax.Precision.HIGHEST)
        hit = jnp.sum(picker, axis=0) > 0.5
        pos, vel, acc, jerk = correct(pos, vel, acc, jerk, spread[0:3], spread[3:6], stride, hit)
        clock = jnp.where(hit, now, clock)
    return (pos, vel, acc, jerk, jnp.stack(recorded))


def solution(mesh):
    in_specs = (
        P(None, ("blk", "grp")),
        P(None, ("blk", "grp")),
        P(None, ("blk", "grp")),
        P(None, ("blk", "grp")),
        P(("blk", "grp")),
        P(("blk", "grp")),
        P(None, ("blk", "grp")),
        P(None, ("blk", "grp")),
    )
    out_specs = (
        P(None, ("blk", "grp")),
        P(None, ("blk", "grp")),
        P(None, ("blk", "grp")),
        P(None, ("blk", "grp")),
        P(None, None, ("blk", "grp")),
    )
    return jax.shard_map(body, mesh=mesh, in_specs=in_specs, out_specs=out_specs, check_vma=False)
```

profile of v0, /device:TPU:0, one launch (start us, length us, event | category | flops | bytes accessed | tf_op | source)
XLA Modules:
  0.0 174.8 jit_solution(9278672865892406174)
XLA Ops:
  0.6 0.7 broadcast_multiply_fusion
  1.3 0.7 multiply_add_fusion.5
  2.1 3.0 %collective-permute-start = (f32[7,256]{1,0:T(8,128)S(1)}, f32[7,256]{1,0:T(8,128)S(1)}, u32[]{:S(2)}, u32[]{:S(2)}) collective-permute-start(f32[7,256]{1,0:T(8,128)S(1)} %pad_maximum_fusion.1), channel_id=1, source_target_pairs={{0,16},{16,0},{1,17},{17,1},{2,18},{18,2},{3,19},{19,3},{4,20},{20... | collective-permute-start | bytes 21512 | tf_op jit(solution)/shard_map/ppermute | solution.py:13
  5.1 0.8 slice_bitcast_fusion.1
  5.9 1.3 fusion.52
  7.2 0.6 iota_compare_fusion.2
  7.8 0.1 convert_reduce_fusion
  7.9 0.2 convolution_bitcast_fusion.1
  8.1 0.7 iota_compare_fusion.3
  8.8 0.7 convert_multiply_fusion
  9.5 21.8 %all-gather = f32[16,24,6]{1,2,0:T(8,128)S(1)} all-gather(f32[1,24,6]{1,2,0:T(8,128)S(1)} %convolution_bitcast_fusion.1), channel_id=1, replica_groups=mesh['blk'=2,'grp'=16] {'grp'}, dimensions={0}, use_global_device_ids=true | all-gather | bytes 9792 | tf_op jit(solution)/shard_map/all_gather | solution.py:77
  31.3 0.1 reshape.72
  31.4 0.1 convert_reduce_fusion.1
  31.5 1.2 dynamic-slice
  33.4 0.0 collective-permute-done
  33.4 0.5 broadcast_subtract_fusion.4
  33.9 0.2 fusion.1
  34.1 0.2 fusion.2
  34.4 0.0 copy-start
  34.4 0.0 copy-start.1
  34.4 0.0 copy-start.2
  34.4 0.0 copy-start.3
  34.4 1.0 multiply_reduce_fusion.7
  35.4 57.8 %all-reduce = f32[6,384]{1,0:T(8,128)S(1)} all-reduce(f32[6,384]{1,0:T(8,128)S(1)} %maximum_add_fusion), channel_id=2, replica_groups=mesh['blk'=2,'grp'=16] {'grp'}, use_global_device_ids=true, to_apply=%region_6.7.clone | all-reduce | flops 2304 | bytes 18432
  93.3 0.2 fusion.25
  93.5 0.0 copy-done
  93.5 0.0 copy-done.1
  93.5 0.0 copy-done.2
  93.5 0.0 copy-done.3
  93.5 0.2 convolution_bitcast_fusion
  93.8 0.6 collective-permute-start.1
  94.3 17.3 %all-gather.1 = f32[16,24,6]{1,2,0:T(8,128)S(1)} all-gather(f32[1,24,6]{1,2,0:T(8,128)S(1)} %convolution_bitcast_fusion), channel_id=1, replica_groups=mesh['blk'=2,'grp'=16] {'grp'}, dimensions={0}, use_global_device_ids=true | all-gather | bytes 9792 | tf_op jit(solution)/shard_map/all_gather | solution.py:77
  111.6 0.1 reshape.74
  111.7 0.1 select_bitcast_fusion.1
  111.8 0.0 collective-permute-done.1
  111.8 0.3 broadcast_subtract_fusion
  112.1 0.3 broadcast_subtract_fusion.1
  112.4 0.2 fusion.5
  112.6 0.2 fusion.6
  112.9 1.0 multiply_reduce_fusion.3
  113.9 59.4 %all-reduce.1 = f32[6,384]{1,0:T(8,128)S(1)} all-reduce(f32[6,384]{1,0:T(8,128)S(1)} %maximum_add_fusion.1), channel_id=3, replica_groups=mesh['blk'=2,'grp'=16] {'grp'}, use_global_device_ids=true, to_apply=%region_11.12.clone | all-reduce | flops 2304 | bytes 18432
  173.3 0.1 select_bitcast_fusion
  173.4 0.2 fusion.21
  173.6 0.6 copy.22
  174.2 0.6 broadcast_select_fusion.1
  (17 shorter events, 0.2 us)
Async XLA Ops:
  2.1 31.3 %collective-permute-start = (f32[7,256]{1,0:T(8,128)S(1)}, f32[7,256]{1,0:T(8,128)S(1)}, u32[]{:S(2)}, u32[]{:S(2)}) collective-permute-start(f32[7,256]{1,0:T(8,128)S(1)} %pad_maximum_fusion.1), channel_id=1, source_target_pairs={{0,16},{16,0},{1,17},{17,1},{2,18},{18,2},{3,19},{19,3},{4,20},{20... | collective-permute-start | bytes 21512 | tf_op jit(solution)/shard_map/ppermute | solution.py:13
  34.4 59.1 %copy-start = (f32[3,256]{1,0:T(4,128)S(1)}, f32[3,256]{1,0:T(4,128)}, u32[]{:S(2)}) copy-start(f32[3,256]{1,0:T(4,128)} %param.11) | copy-start | bytes 9220
  34.4 59.1 %copy-start.1 = (f32[3,256]{1,0:T(4,128)S(1)}, f32[3,256]{1,0:T(4,128)}, u32[]{:S(2)}) copy-start(f32[3,256]{1,0:T(4,128)} %param.8) | copy-start | bytes 9220
  34.4 59.1 %copy-start.2 = (f32[3,256]{1,0:T(4,128)S(1)}, f32[3,256]{1,0:T(4,128)}, u32[]{:S(2)}) copy-start(f32[3,256]{1,0:T(4,128)} %param.9) | copy-start | bytes 9220
  34.4 59.1 %copy-start.3 = (f32[3,256]{1,0:T(4,128)S(1)}, f32[3,256]{1,0:T(4,128)}, u32[]{:S(2)}) copy-start(f32[3,256]{1,0:T(4,128)} %param.10) | copy-start | bytes 9220
  93.8 18.0 %collective-permute-start.1 = (f32[7,256]{1,0:T(8,128)S(1)}, f32[7,256]{1,0:T(8,128)S(1)}, u32[]{:S(2)}, u32[]{:S(2)}) collective-permute-start(f32[7,256]{1,0:T(8,128)S(1)} %pad_maximum_fusion), channel_id=1, source_target_pairs={{0,16},{16,0},{1,17},{17,1},{2,18},{18,2},{3,19},{19,3},{4,20},{20... | collective-permute-start | bytes 21512 | tf_op jit(solution)/shard_map/ppermute | solution.py:13
where the time goes:
time: 175 us
  blocking collectives  156 us (89%)
  other arithmetic  8.46 us (5%)
  local copies, waits for them, and re-layouts  4.17 us (2%)
  starting transfers between devices  3.6 us (2%)
    unnamed x2, blocking collectives  117 us
    all_gather x2, blocking collectives, body(): row_actives = lax.all_gather(chosen, 'grp', axis=1, tiled=True)  39 us
    ppermute x2, starting transfers between devices, passed_along(): return lax.ppermute(value, axis, pairs)  3.6 us
  transfers between devices with their start and end apart: 2, of which 0 were waited for; matrix products, arithmetic and copies ran while one was open for 3% of the time, Pallas kernels for 0%

commit v1 on v0

v1 whole, which is shorter than its diff:
```python
import functools
import math

import jax
import jax.numpy as jnp
from jax import lax
from jax.experimental import pallas as pl
from jax.experimental.pallas import tpu as pltpu
from jax.sharding import PartitionSpec as P

STEP_BASE = 0.125
SOFTEN = 0.01
LANES = 128
MESH = pl.DeviceIdType.MESH


def predict(pos, vel, acc, jerk, elapsed):
    pred_pos = pos + elapsed * (vel + elapsed * (acc * 0.5 + elapsed * jerk / 6.0))
    pred_vel = vel + elapsed * (acc + elapsed * jerk * 0.5)
    return (pred_pos, pred_vel)


def correct(pos, vel, acc, jerk, new_acc, new_jerk, stride, hit):
    half = 0.5 * stride
    square = stride * stride / 12.0
    vel_new = vel + half * (acc + new_acc) + square * (jerk - new_jerk)
    pos_new = pos + half * (vel + vel_new) + square * (acc - new_acc)
    return (
        jnp.where(hit, pos_new, pos),
        jnp.where(hit, vel_new, vel),
        jnp.where(hit, new_acc, acc),
        jnp.where(hit, new_jerk, jerk),
    )


def add_pairs(target, source, total):
    dpos = [source[c] - target[c] for c in range(3)]
    dvel = [source[c + 3] - target[c + 3] for c in range(3)]
    dist = dpos[0] * dpos[0] + dpos[1] * dpos[1] + dpos[2] * dpos[2] + SOFTEN
    inverse = lax.rsqrt(dist)
    square = inverse * inverse
    weight = source[6] * (inverse * square)
    radial = (3.0 * square) * (dpos[0] * dvel[0] + dpos[1] * dvel[1] + dpos[2] * dvel[2])
    accel = [total[c] + weight * dpos[c] for c in range(3)]
    jerk = [total[c + 3] + weight * (dvel[c] - radial * dpos[c]) for c in range(3)]
    return tuple(accel + jerk)


def kernel(
    n_blk, n_grp, act,
    pos_h, vel_h, acc_h, jerk_h, mass_h, lev_h, lists_h, counts_h,
    pos_o, vel_o, acc_o, jerk_o, fresh_o,
    pos_v, vel_v, acc_v, jerk_v, mass_v, lev_v, lists_v, counts_v,
    src1, src2, extra, tgt1, tgt2, part1, part2,
    load_sem, bulk_send, bulk_recv, pair_send, pair_recv,
):
    blk, grp = lax.axis_index("blk"), lax.axis_index("grp")
    per_blk = n_grp // 2
    chips = n_blk * per_blk
    core = lax.rem(grp, 2)
    chip = blk * per_blk + grp // 2
    partner = (blk, grp + 1 - 2 * core)
    part_dev = pos_h.shape[1]
    total_part = part_dev * n_blk * n_grp
    width = 1 << (act - 1).bit_length()
    group = math.gcd(LANES // width, chips)

    def chip_at(k):
        there = lax.rem(chip + k, chips)
        return (there // per_blk, 2 * lax.rem(there, per_blk) + core)

    loads = [
        pltpu.make_async_copy(h, v, load_sem.at[i])
        for i, (h, v) in enumerate(
            [(pos_h, pos_v), (vel_h, vel_v), (acc_h, acc_v), (jerk_h, jerk_v),
             (mass_h, mass_v), (lev_h, lev_v), (lists_h, lists_v), (counts_h, counts_v)]
        )
    ]
    for load in loads:
        load.start()

    barrier = pltpu.get_barrier_semaphore()

    def greet(k, carry):
        pl.semaphore_signal(barrier, inc=1, device_id=chip_at(k), device_id_type=MESH)
        return carry

    lax.fori_loop(1, chips, greet, 0)
    pl.semaphore_signal(barrier, inc=1, device_id=partner, device_id_type=MESH)

    def send_bulk(buffer, which):
        def send(k, carry):
            pltpu.make_async_remote_copy(
                src_ref=buffer.at[0], dst_ref=buffer.at[k],
                send_sem=bulk_send.at[which], recv_sem=bulk_recv.at[which],
                device_id=chip_at(k), device_id_type=MESH,
            ).start()
            return carry

        lax.fori_loop(1, chips, send, 0)

    def whole_bulk(buffer, which):
        others = buffer.at[pl.ds(1, chips - 1)]
        return pltpu.make_async_remote_copy(
            src_ref=others, dst_ref=others,
            send_sem=bulk_send.at[which], recv_sem=bulk_recv.at[which],
            device_id=partner, device_id_type=MESH,
        )

    def pair_copy(buffer, which):
        return pltpu.make_async_remote_copy(
            src_ref=buffer.at[0], dst_ref=buffer.at[1],
            send_sem=pair_send.at[which], recv_sem=pair_recv.at[which],
            device_id=partner, device_id_type=MESH,
        )

    for load in loads:
        load.wait()
    pos, vel, acc, jerk = pos_v[...], vel_v[...], acc_v[...], jerk_v[...]
    mass = mass_v[...] / total_part
    levels = lev_v[...]
    stride = STEP_BASE * jnp.left_shift(jnp.ones_like(levels), levels).astype(jnp.float32)
    hit_one, hit_two = levels == 0, levels <= 1
    pred_pos, pred_vel = predict(pos, vel, acc, jerk, STEP_BASE)
    src1[0, 0:3, :] = pred_pos
    src1[0, 3:6, :] = pred_vel
    src1[0, 6:7, :] = mass
    src1[0, 7:8, :] = jnp.zeros_like(mass)

    pl.semaphore_wait(barrier, chips)
    send_bulk(src1, 0)

    sub_row = lax.broadcasted_iota(jnp.int32, (act, LANES), 0)
    lane = lax.broadcasted_iota(jnp.int32, (act, LANES), 1)
    particle = lax.broadcasted_iota(jnp.int32, (act, part_dev), 1)
    count_one = jnp.broadcast_to(counts_v[0:1, :], (act, LANES))
    count_two = jnp.broadcast_to(counts_v[1:2, :], (act, LANES))
    list_one = jnp.concatenate([lists_v[0:1, :], jnp.zeros((1, LANES - act), jnp.int32)], axis=1)
    list_two = jnp.concatenate([lists_v[1:2, :], jnp.zeros((1, LANES - act), jnp.int32)], axis=1)
    shift = core * (act - count_one)
    place_one = (lane == sub_row - shift) & (lane < count_one)
    place_two = (lane == sub_row) & (lane < count_two)

    def picker_of(place, row):
        value = jnp.where(place, (row + 1).astype(jnp.float32), 0.0)
        column = jnp.sum(value, axis=1, keepdims=True) - 1.0
        return particle.astype(jnp.float32) == column

    def picked(picker, rows):
        return jnp.sum(jnp.where(picker, rows, 0.0), axis=1, keepdims=True)

    def packed(columns):
        tile = jnp.zeros((act, LANES), jnp.float32)
        for c, column in enumerate(columns):
            tile = jnp.where(lane == c, column, tile)
        return tile

    def spread(mask, tile):
        return [
            jnp.sum(jnp.where(mask, tile[:, c : c + 1], 0.0), axis=0, keepdims=True)
            for c in range(6)
        ]

    def targets_of(tile):
        return [jnp.broadcast_to(tile[:, c : c + 1], (act, LANES)) for c in range(6)]

    def zeros():
        return tuple(jnp.zeros((act, LANES), jnp.float32) for _ in range(6))

    def over_bulk(targets, buffer, total):
        def slot(k, total):
            for start in range(0, part_dev, LANES):
                rows = [buffer[k, c : c + 1, start : start + LANES] for c in range(7)]
                total = add_pairs(targets, rows, total)
            return total

        return lax.fori_loop(0, chips, slot, total)

    def over_extra(targets, total):
        def chunk(g, total):
            tile = extra[g * group]
            for i in range(1, group):
                tile = tile + extra[g * group + i]
            return add_pairs(targets, [tile[c : c + 1] for c in range(7)], total)

        return lax.fori_loop(0, chips // group, chunk, total)

    def reduced(total):
        return packed([jnp.sum(part, axis=1, keepdims=True) for part in total])

    picker_one = picker_of(place_one, list_one)
    tgt1[0] = packed(
        [picked(picker_one, pred_pos[c : c + 1]) for c in range(3)]
        + [picked(picker_one, pred_vel[c : c + 1]) for c in range(3)]
    )
    to_pair_one = pair_copy(tgt1, 0)
    to_pair_one.start()
    late_pos, late_vel = predict(pos, vel, acc, jerk, 2 * STEP_BASE)
    src2[0, 0:3, :] = late_pos
    src2[0, 3:6, :] = late_vel
    src2[0, 6:7, :] = jnp.where(hit_one, 0.0, mass)
    src2[0, 7:8, :] = jnp.zeros_like(mass)
    send_bulk(src2, 1)
    picker_two = picker_of(place_two, list_two)
    to_pair_one.wait_recv()
    targets = targets_of(tgt1[0] + tgt1[1])
    whole_bulk(src1, 0).wait_recv()
    part1[0] = reduced(over_bulk(targets, src1, zeros()))
    sums_one = pair_copy(part1, 1)
    sums_one.start()
    sums_one.wait_recv()
    force_one = part1[0] + part1[1]
    rows = spread(picker_one, force_one)
    new_acc, new_jerk = jnp.concatenate(rows[0:3], axis=0), jnp.concatenate(rows[3:6], axis=0)
    pos, vel, acc, jerk = correct(pos, vel, acc, jerk, new_acc, new_jerk, stride, hit_one)

    elapsed = jnp.where(hit_one, STEP_BASE, 2 * STEP_BASE)
    pred_pos, pred_vel = predict(pos, vel, acc, jerk, elapsed)
    columns = (
        [picked(picker_two, pred_pos[c : c + 1]) for c in range(3)]
        + [picked(picker_two, pred_vel[c : c + 1]) for c in range(3)]
        + [picked(picker_two, jnp.where(hit_one, mass, 0.0))]
    )
    offset = lax.rem(chip, group) * width
    window = lane == sub_row + offset
    for c, column in enumerate(columns):
        extra[0, c : c + 1, :] = jnp.sum(jnp.where(window, column, 0.0), axis=0, keepdims=True)
    extra[0, 7:8, :] = jnp.zeros((1, LANES), jnp.float32)
    send_bulk(extra, 2)
    tgt2[0] = packed(columns[0:6])
    to_pair_two = pair_copy(tgt2, 2)
    to_pair_two.start()
    for c, row in enumerate(spread(place_one, force_one)):
        fresh_o[0, c : c + 1, :] = row[:, 0:act]

    whole_bulk(src2, 1).wait_recv()
    own_total = over_bulk([jnp.broadcast_to(c, (act, LANES)) for c in columns[0:6]], src2, zeros())
    part2[2] = reduced(own_total)
    to_pair_two.wait_recv()
    targets = targets_of(tgt2[1])
    total = over_bulk(targets, src2, zeros())
    whole_bulk(extra, 2).wait_recv()
    part2[0] = reduced(over_extra(targets, total))
    sums_two = pair_copy(part2, 3)
    sums_two.start()
    own_extra = reduced(over_extra(targets_of(tgt2[0]), zeros()))
    own = part2[2] + own_extra
    sums_two.wait_recv()
    force_two = own + part2[1]
    rows = spread(picker_two, force_two)
    new_acc, new_jerk = jnp.concatenate(rows[0:3], axis=0), jnp.concatenate(rows[3:6], axis=0)
    pos, vel, acc, jerk = correct(pos, vel, acc, jerk, new_acc, new_jerk, stride, hit_two)
    pos_o[...] = pos
    vel_o[...] = vel
    acc_o[...] = acc
    jerk_o[...] = jerk
    for c, row in enumerate(spread(place_two, force_two)):
        fresh_o[1, c : c + 1, :] = row[:, 0:act]

    for which, buffer in enumerate((src1, src2, extra)):
        whole_bulk(buffer, which).wait_send()
    for copy in (to_pair_one, sums_one, to_pair_two, sums_two):
        copy.wait_send()


def body(n_blk, n_grp, positions, velocities, accelerations, jerks, mass_weight, levels, active, counts):
    part_dev, act = positions.shape[1], active.shape[1]
    chips = n_blk * n_grp // 2
    state = jax.ShapeDtypeStruct((3, part_dev), jnp.float32)
    vmem = pltpu.VMEM
    return pl.pallas_call(
        functools.partial(kernel, n_blk, n_grp, act),
        out_shape=(state, state, state, state, jax.ShapeDtypeStruct((2, 6, act), jnp.float32)),
        in_specs=[pl.BlockSpec(memory_space=pl.ANY)] * 8,
        out_specs=[pl.BlockSpec(memory_space=vmem)] * 5,
        scratch_shapes=[
            vmem((3, part_dev), jnp.float32),
            vmem((3, part_dev), jnp.float32),
            vmem((3, part_dev), jnp.float32),
            vmem((3, part_dev), jnp.float32),
            vmem((1, part_dev), jnp.float32),
            vmem((1, part_dev), jnp.int32),
            vmem((2, act), jnp.int32),
            vmem((2, 1), jnp.int32),
            vmem((chips, 8, part_dev), jnp.float32),
            vmem((chips, 8, part_dev), jnp.float32),
            vmem((chips, 8, LANES), jnp.float32),
            vmem((2, act, LANES), jnp.float32),
            vmem((2, act, LANES), jnp.float32),
            vmem((2, act, LANES), jnp.float32),
            vmem((3, act, LANES), jnp.float32),
            pltpu.SemaphoreType.DMA((8,)),
            pltpu.SemaphoreType.DMA((3,)),
            pltpu.SemaphoreType.DMA((3,)),
            pltpu.SemaphoreType.DMA((4,)),
            pltpu.SemaphoreType.DMA((4,)),
        ],
        compiler_params=pltpu.CompilerParams(
            collective_id=0, has_side_effects=True, vmem_limit_bytes=32 * 1024 * 1024
        ),
    )(
        positions, velocities, accelerations, jerks,
        mass_weight.reshape(1, part_dev), levels.reshape(1, part_dev), active, counts,
    )


def solution(mesh):
    spread_over = ("blk", "grp")
    in_specs = (
        P(None, spread_over),
        P(None, spread_over),
        P(None, spread_over),
        P(None, spread_over),
        P(spread_over),
        P(spread_over),
        P(None, spread_over),
        P(None, spread_over),
    )
    out_specs = (
        P(None, spread_over),
        P(None, spread_over),
        P(None, spread_over),
        P(None, spread_over),
        P(None, None, spread_over),
    )
    inner = functools.partial(body, mesh.shape["blk"], mesh.shape["grp"])
    return jax.shard_map(inner, mesh=mesh, in_specs=in_specs, out_specs=out_specs, check_vma=False)
```

time: 175 us -> 28.9 us (0.17)
  blocking collectives: 156 us -> 0 us
  Pallas kernels: 0 us -> 20.8 us
  other arithmetic: 8.46 us -> 0 us
  starting transfers between devices: 3.6 us -> 0 us
  local copies, waits for them, and re-layouts: 4.17 us -> 7.14 us
    unnamed x2 -> x0, blocking collectives: 117 us -> none
    all_gather x2 -> x0, blocking collectives: 39 us -> none  [body(): row_actives = lax.all_gather(chosen, 'grp', axis=1, tiled=True)]
    pallas_call x0 -> x1, Pallas kernels: none -> 20.8 us  [body(): pl.pallas_call(functools.partial(kernel, n_blk, n_grp, act), out_shape=(s...]
    unnamed x12 -> x19, local copies, waits for them, and re-layouts: 2.05 us -> 6.55 us
    ppermute x2 -> x0, starting transfers between devices: 3.6 us -> none  [passed_along(): return lax.ppermute(value, axis, pairs)]
    reduce_sum x4 -> x0, other arithmetic: 2.18 us -> none  [the longest x2 2 us: block_terms(): accel = jnp.sum(weight[None] * dpos, axis=1)]
  transfers between devices with their start and end apart: 2 -> 0, of which waited for: 0 -> 0; matrix products, arithmetic and copies ran while one was open for 3% -> 0% of each run, Pallas kernels for 0% -> 0%
where the time goes in v1:
time: 28.9 us; the launch traced here: 28.6 us
  Pallas kernels  20.8 us (72%)
  local copies, waits for them, and re-layouts  7.14 us (25%)
  between operations  0.66 us (2%)
    pallas_call x1, Pallas kernels, body(): pl.pallas_call(functools.partial(kernel, n_blk, n_grp, act), out_shape=(s...  20.8 us
    unnamed x19, local copies, waits for them, and re-layouts  6.55 us
    pallas_call x1, local copies, waits for them, and re-layouts, body(): pl.pallas_call(functools.partial(kernel, n_blk, n_grp, act), out_shape=(s...  0.6 us

profile of v1, /device:TPU:0, one launch (start us, length us, event | category | flops | bytes accessed | tf_op | source)
XLA Modules:
  0.0 28.6 jit_solution(7408640795869782829)
XLA Ops:
  0.6 0.0 copy-start
  0.6 0.0 copy-start.4
  0.7 0.8 %copy.13.counts_h = s32[2,1]{1,0:T(2,128)S(1)} copy(s32[2,1]{0,1:T(1,128)} %param.15) | data formatting | bytes 16 | tf_op args[7]
  1.4 0.0 copy-done
  1.4 0.0 copy-done.4
  1.4 0.0 copy-start.1
  1.4 0.7 %copy-done.1 = f32[3,256]{1,0:T(4,128)S(1)} copy-done((f32[3,256]{1,0:T(4,128)S(1)}, f32[3,256]{1,0:T(4,128)}, u32[]{:S(2)}) %copy-start.1) | copy-done | bytes 3096
  2.1 0.0 copy-start.2
  2.1 0.7 %copy-done.2 = f32[3,256]{1,0:T(4,128)S(1)} copy-done((f32[3,256]{1,0:T(4,128)S(1)}, f32[3,256]{1,0:T(4,128)}, u32[]{:S(2)}) %copy-start.2) | copy-done | bytes 3096
  2.8 0.0 copy-start.3
  2.8 0.7 %copy-done.3 = f32[3,256]{1,0:T(4,128)S(1)} copy-done((f32[3,256]{1,0:T(4,128)S(1)}, f32[3,256]{1,0:T(4,128)}, u32[]{:S(2)}) %copy-start.3) | copy-done | bytes 3096
  3.5 0.0 copy-start.5
  3.5 0.7 %copy-done.5 = s32[256]{0:T(256)S(1)} copy-done((s32[256]{0:T(256)S(1)}, s32[256]{0:T(256)}, u32[]{:S(2)}) %copy-start.5) | copy-done | bytes 1048
  4.2 0.0 copy-start.6
  4.2 0.7 %copy-done.6 = s32[2,24]{1,0:T(2,128)S(1)} copy-done((s32[2,24]{1,0:T(2,128)S(1)}, s32[2,24]{1,0:T(2,128)}, u32[]{:S(2)}) %copy-start.6) | copy-done | bytes 216
  4.8 20.8 %shard_map.119 = (f32[3,256]{1,0:T(4,128)S(1)}, f32[3,256]{1,0:T(4,128)S(1)}, f32[3,256]{1,0:T(4,128)S(1)}, f32[3,256]{1,0:T(4,128)S(1)}, f32[2,6,24]{2,1,0:T(8,128)S(1)}) custom-call(f32[3,256]{1,0:T(4,128)S(1)} %copy-done, f32[3,256]{1,0:T(4,128)S(1)} %copy-done.1, f32[3,256]{1,0:T(4,128)S(1)} %copy-done.2, f32[3,256]{1,0:T(4,128)S(1)} %copy-done.3, ...), custom_call_target="tpu_custom_call" | custom-call | tf_op jit(solution)/shard_map/pallas_call | solution.py:271
  25.6 0.6 %copy.14 = f32[2,6,24]{2,0,1:T(2,128)} copy(f32[2,6,24]{2,1,0:T(8,128)S(1)} %get-tuple-element.9) | data formatting | bytes 2304 | tf_op jit(solution)/shard_map/pallas_call | solution.py:271
  26.2 0.6 %copy.19 = f32[3,256]{1,0:T(4,128)} copy(f32[3,256]{1,0:T(4,128)S(1)} %get-tuple-element.15) | data formatting | bytes 6144
  26.8 0.6 %copy.20 = f32[3,256]{1,0:T(4,128)} copy(f32[3,256]{1,0:T(4,128)S(1)} %get-tuple-element.16) | data formatting | bytes 6144
  27.4 0.6 %copy.21 = f32[3,256]{1,0:T(4,128)} copy(f32[3,256]{1,0:T(4,128)S(1)} %get-tuple-element.17) | data formatting | bytes 6144
  28.0 0.6 %copy.22 = f32[3,256]{1,0:T(4,128)} copy(f32[3,256]{1,0:T(4,128)S(1)} %get-tuple-element.18) | data formatting | bytes 6144
Async XLA Ops:
  0.6 0.8 %copy-start = (f32[3,256]{1,0:T(4,128)S(1)}, f32[3,256]{1,0:T(4,128)}, u32[]{:S(2)}) copy-start(f32[3,256]{1,0:T(4,128)} %pos_h.1) | copy-start | bytes 9220
  0.6 0.8 %copy-start.4 = (f32[256]{0:T(256)S(1)}, f32[256]{0:T(256)}, u32[]{:S(2)}) copy-start(f32[256]{0:T(256)} %param.12) | copy-start | bytes 3076
  1.4 0.7 %copy-start.1 = (f32[3,256]{1,0:T(4,128)S(1)}, f32[3,256]{1,0:T(4,128)}, u32[]{:S(2)}) copy-start(f32[3,256]{1,0:T(4,128)} %vel_h.1) | copy-start | bytes 9220
  2.1 0.7 %copy-start.2 = (f32[3,256]{1,0:T(4,128)S(1)}, f32[3,256]{1,0:T(4,128)}, u32[]{:S(2)}) copy-start(f32[3,256]{1,0:T(4,128)} %acc_h.1) | copy-start | bytes 9220
  2.8 0.7 %copy-start.3 = (f32[3,256]{1,0:T(4,128)S(1)}, f32[3,256]{1,0:T(4,128)}, u32[]{:S(2)}) copy-start(f32[3,256]{1,0:T(4,128)} %jerk_h.1) | copy-start | bytes 9220
  3.5 0.7 %copy-start.5 = (s32[256]{0:T(256)S(1)}, s32[256]{0:T(256)}, u32[]{:S(2)}) copy-start(s32[256]{0:T(256)} %param.13) | copy-start | bytes 3076
  4.2 0.7 %copy-start.6 = (s32[2,24]{1,0:T(2,128)S(1)}, s32[2,24]{1,0:T(2,128)}, u32[]{:S(2)}) copy-start(s32[2,24]{1,0:T(2,128)} %lists_h.1) | copy-start | bytes 580

commit v2 on v1

--- a/solution.py
+++ b/solution.py
@@ -76,8 +76,6 @@
              (mass_h, mass_v), (lev_h, lev_v), (lists_h, lists_v), (counts_h, counts_v)]
         )
     ]
-    for load in loads:
-        load.start()
 
     barrier = pltpu.get_barrier_semaphore()
 
@@ -87,25 +85,34 @@
 
     lax.fori_loop(1, chips, greet, 0)
     pl.semaphore_signal(barrier, inc=1, device_id=partner, device_id_type=MESH)
+    for load in loads:
+        load.start()
 
     def send_bulk(buffer, which):
         def send(k, carry):
             pltpu.make_async_remote_copy(
                 src_ref=buffer.at[0], dst_ref=buffer.at[k],
-                send_sem=bulk_send.at[which], recv_sem=bulk_recv.at[which],
+                send_sem=bulk_send.at[which], recv_sem=bulk_recv.at[which, k // group],
                 device_id=chip_at(k), device_id_type=MESH,
             ).start()
             return carry
 
         lax.fori_loop(1, chips, send, 0)
 
-    def whole_bulk(buffer, which):
-        others = buffer.at[pl.ds(1, chips - 1)]
+    def arrival(buffer, which, first, count, sems):
+        others = buffer.at[pl.ds(first, count)]
         return pltpu.make_async_remote_copy(
             src_ref=others, dst_ref=others,
-            send_sem=bulk_send.at[which], recv_sem=bulk_recv.at[which],
+            send_sem=bulk_send.at[which], recv_sem=bulk_recv.at[which, sems],
             device_id=partner, device_id_type=MESH,
         )
+
+    def await_group(buffer, which, g):
+        if isinstance(g, int) and g == 0:
+            if group > 1:
+                arrival(buffer, which, 1, group - 1, 0).wait_recv()
+        else:
+            arrival(buffer, which, g * group, group, g).wait_recv()
 
     def pair_copy(buffer, which):
         return pltpu.make_async_remote_copy(
@@ -127,14 +134,11 @@
     src1[0, 6:7, :] = mass
     src1[0, 7:8, :] = jnp.zeros_like(mass)
 
-    pl.semaphore_wait(barrier, chips)
-    send_bulk(src1, 0)
-
     sub_row = lax.broadcasted_iota(jnp.int32, (act, LANES), 0)
     lane = lax.broadcasted_iota(jnp.int32, (act, LANES), 1)
     particle = lax.broadcasted_iota(jnp.int32, (act, part_dev), 1)
-    count_one = jnp.broadcast_to(counts_v[0:1, :], (act, LANES))
-    count_two = jnp.broadcast_to(counts_v[1:2, :], (act, LANES))
+    count_one = jnp.broadcast_to(counts_v[0:1, 0:1], (act, LANES))
+    count_two = jnp.broadcast_to(counts_v[0:1, 1:2], (act, LANES))
     list_one = jnp.concatenate([lists_v[0:1, :], jnp.zeros((1, LANES - act), jnp.int32)], axis=1)
     list_two = jnp.concatenate([lists_v[1:2, :], jnp.zeros((1, LANES - act), jnp.int32)], axis=1)
     shift = core * (act - count_one)
@@ -167,23 +171,29 @@
     def zeros():
         return tuple(jnp.zeros((act, LANES), jnp.float32) for _ in range(6))
 
-    def over_bulk(targets, buffer, total):
-        def slot(k, total):
-            for start in range(0, part_dev, LANES):
-                rows = [buffer[k, c : c + 1, start : start + LANES] for c in range(7)]
-                total = add_pairs(targets, rows, total)
+    def over_bulk(targets, buffer, total, which=None):
+        def some(g, total):
+            if which is not None:
+                await_group(buffer, which, g)
+            for i in range(group):
+                for start in range(0, part_dev, LANES):
+                    k = g * group + i
+                    rows = [buffer[k, c : c + 1, start : start + LANES] for c in range(7)]
+                    total = add_pairs(targets, rows, total)
             return total
 
-        return lax.fori_loop(0, chips, slot, total)
-
-    def over_extra(targets, total):
+        return lax.fori_loop(1, chips // group, some, some(0, total))
+
+    def over_extra(targets, total, which=None):
         def chunk(g, total):
+            if which is not None:
+                await_group(extra, which, g)
             tile = extra[g * group]
             for i in range(1, group):
                 tile = tile + extra[g * group + i]
             return add_pairs(targets, [tile[c : c + 1] for c in range(7)], total)
 
-        return lax.fori_loop(0, chips // group, chunk, total)
+        return lax.fori_loop(1, chips // group, chunk, chunk(0, total))
 
     def reduced(total):
         return packed([jnp.sum(part, axis=1, keepdims=True) for part in total])
@@ -193,19 +203,20 @@
         [picked(picker_one, pred_pos[c : c + 1]) for c in range(3)]
         + [picked(picker_one, pred_vel[c : c + 1]) for c in range(3)]
     )
-    to_pair_one = pair_copy(tgt1, 0)
-    to_pair_one.start()
     late_pos, late_vel = predict(pos, vel, acc, jerk, 2 * STEP_BASE)
     src2[0, 0:3, :] = late_pos
     src2[0, 3:6, :] = late_vel
     src2[0, 6:7, :] = jnp.where(hit_one, 0.0, mass)
     src2[0, 7:8, :] = jnp.zeros_like(mass)
+    picker_two = picker_of(place_two, list_two)
+    pl.semaphore_wait(barrier, chips)
+    to_pair_one = pair_copy(tgt1, 0)
+    to_pair_one.start()
+    send_bulk(src1, 0)
     send_bulk(src2, 1)
-    picker_two = picker_of(place_two, list_two)
     to_pair_one.wait_recv()
     targets = targets_of(tgt1[0] + tgt1[1])
-    whole_bulk(src1, 0).wait_recv()
-    part1[0] = reduced(over_bulk(targets, src1, zeros()))
+    part1[0] = reduced(over_bulk(targets, src1, zeros(), 0))
     sums_one = pair_copy(part1, 1)
     sums_one.start()
     sums_one.wait_recv()
@@ -231,16 +242,14 @@
     to_pair_two = pair_copy(tgt2, 2)
     to_pair_two.start()
     for c, row in enumerate(spread(place_one, force_one)):
-        fresh_o[0, c : c + 1, :] = row[:, 0:act]
-
-    whole_bulk(src2, 1).wait_recv()
-    own_total = over_bulk([jnp.broadcast_to(c, (act, LANES)) for c in columns[0:6]], src2, zeros())
+        fresh_o[c, 0:1, :] = row[:, 0:act]
+
+    own_total = over_bulk([jnp.broadcast_to(c, (act, LANES)) for c in columns[0:6]], src2, zeros(), 1)
     part2[2] = reduced(own_total)
     to_pair_two.wait_recv()
     targets = targets_of(tgt2[1])
     total = over_bulk(targets, src2, zeros())
-    whole_bulk(extra, 2).wait_recv()
-    part2[0] = reduced(over_extra(targets, total))
+    part2[0] = reduced(over_extra(targets, total, 2))
     sums_two = pair_copy(part2, 3)
     sums_two.start()
     own_extra = reduced(over_extra(targets_of(tgt2[0]), zeros()))
@@ -255,23 +264,32 @@
     acc_o[...] = acc
     jerk_o[...] = jerk
     for c, row in enumerate(spread(place_two, force_two)):
-        fresh_o[1, c : c + 1, :] = row[:, 0:act]
+        fresh_o[c, 1:2, :] = row[:, 0:act]
 
     for which, buffer in enumerate((src1, src2, extra)):
-        whole_bulk(buffer, which).wait_send()
+        arrival(buffer, which, 1, chips - 1, 0).wait_send()
     for copy in (to_pair_one, sums_one, to_pair_two, sums_two):
         copy.wait_send()
+
+
+def write_out(*refs):
+    sems = refs[10]
+    copies = [pltpu.make_async_copy(refs[i], refs[5 + i], sems.at[i]) for i in range(5)]
+    for copy in copies:
+        copy.start()
+    for copy in copies:
+        copy.wait()
 
 
 def body(n_blk, n_grp, positions, velocities, accelerations, jerks, mass_weight, levels, active, counts):
     part_dev, act = positions.shape[1], active.shape[1]
     chips = n_blk * n_grp // 2
-    state = jax.ShapeDtypeStruct((3, part_dev), jnp.float32)
+    state = pltpu.VMEM((3, part_dev), jnp.float32)
     vmem = pltpu.VMEM
-    return pl.pallas_call(
+    results = pl.pallas_call(
         functools.partial(kernel, n_blk, n_grp, act),
-        out_shape=(state, state, state, state, jax.ShapeDtypeStruct((2, 6, act), jnp.float32)),
-        in_specs=[pl.BlockSpec(memory_space=pl.ANY)] * 8,
+        out_shape=(state, state, state, state, pltpu.VMEM((6, 2, act), jnp.float32)),
+        in_specs=[pl.BlockSpec(memory_space=pltpu.HBM)] * 8,
         out_specs=[pl.BlockSpec(memory_space=vmem)] * 5,
         scratch_shapes=[
             vmem((3, part_dev), jnp.float32),
@@ -281,7 +299,7 @@
             vmem((1, part_dev), jnp.float32),
             vmem((1, part_dev), jnp.int32),
             vmem((2, act), jnp.int32),
-            vmem((2, 1), jnp.int32),
+            vmem((1, 2), jnp.int32),
             vmem((chips, 8, part_dev), jnp.float32),
             vmem((chips, 8, part_dev), jnp.float32),
             vmem((chips, 8, LANES), jnp.float32),
@@ -291,17 +309,25 @@
             vmem((3, act, LANES), jnp.float32),
             pltpu.SemaphoreType.DMA((8,)),
             pltpu.SemaphoreType.DMA((3,)),
-            pltpu.SemaphoreType.DMA((3,)),
+            pltpu.SemaphoreType.DMA((3, chips)),
             pltpu.SemaphoreType.DMA((4,)),
             pltpu.SemaphoreType.DMA((4,)),
         ],
         compiler_params=pltpu.CompilerParams(
             collective_id=0, has_side_effects=True, vmem_limit_bytes=32 * 1024 * 1024
         ),
-    )(
+    )(*[pltpu.with_memory_space_constraint(value, pltpu.HBM) for value in (
         positions, velocities, accelerations, jerks,
-        mass_weight.reshape(1, part_dev), levels.reshape(1, part_dev), active, counts,
-    )
+        mass_weight.reshape(1, part_dev), levels.reshape(1, part_dev), active, counts.reshape(1, 2),
+    )])
+    written = pl.pallas_call(
+        write_out,
+        out_shape=[jax.ShapeDtypeStruct(r.shape, r.dtype) for r in results],
+        in_specs=[pl.BlockSpec(memory_space=vmem)] * 5,
+        out_specs=[pl.BlockSpec(memory_space=pltpu.HBM)] * 5,
+        scratch_shapes=[pltpu.SemaphoreType.DMA((5,))],
+    )(*results)
+    return (*written[0:4], written[4].transpose(1, 0, 2))
 
 
 def solution(mesh):

time: 28.9 us -> 25.9 us (0.90)
  local copies, waits for them, and re-layouts: 7.14 us -> 2.95 us
  Pallas kernels: 20.8 us -> 22.1 us
    unnamed x19 -> x10, local copies, waits for them, and re-layouts: 6.55 us -> 2.95 us
    pallas_call x0 -> x1, Pallas kernels: none -> 1.36 us  [body(): pl.pallas_call(write_out, out_shape=[jax.ShapeDtypeStruct(r.shape, r.dtyp...]
    pallas_call x1 -> x0, local copies, waits for them, and re-layouts: 0.6 us -> none  [body(): pl.pallas_call(functools.partial(kernel, n_blk, n_grp, act), out_shape=(s...]
where the time goes in v2:
time: 25.9 us; the launch traced here: 25.7 us
  Pallas kernels  22.1 us (85%)
  local copies, waits for them, and re-layouts  2.95 us (11%)
  between operations  0.65 us (3%)
    pallas_call x1, Pallas kernels, body(): pl.pallas_call(functools.partial(kernel, n_blk, n_grp, act), out_shape=(s...  20.7 us
    unnamed x10, local copies, waits for them, and re-layouts  2.95 us
    pallas_call x1, Pallas kernels, body(): pl.pallas_call(write_out, out_shape=[jax.ShapeDtypeStruct(r.shape, r.dtyp...  1.36 us

profile of v2, /device:TPU:0, one launch (start us, length us, event | category | flops | bytes accessed | tf_op | source)
XLA Modules:
  0.0 25.7 jit_solution(6896533403192505603)
XLA Ops:
  0.6 20.7 %shard_map.119 = (f32[3,256]{1,0:T(4,128)S(1)}, f32[3,256]{1,0:T(4,128)S(1)}, f32[3,256]{1,0:T(4,128)S(1)}, f32[3,256]{1,0:T(4,128)S(1)}, f32[6,2,24]{2,1,0:T(2,128)S(1)}) custom-call(f32[3,256]{1,0:T(4,128)} %pos_h.1, f32[3,256]{1,0:T(4,128)} %vel_h.1, f32[3,256]{1,0:T(4,128)} %acc_h.1, f32[3,256]{1,0:T(4,128)} %jerk_h.1, f32[1,256]{1,0:T(1,128)} %bitcast.4, ...), custom_call_target="tpu_custom_call" | custom-call | tf_op jit(solution)/shard_map/pallas_call | solution.py:289
  21.3 0.0 copy-start
  21.4 0.6 %copy-done = f32[6,2,24]{2,1,0:T(2,128)} copy-done((f32[6,2,24]{2,1,0:T(2,128)}, f32[6,2,24]{2,1,0:T(2,128)S(1)}, u32[]{:S(2)}) %copy-start) | copy-done | bytes 1176
  21.9 0.0 copy-start.1
  21.9 0.6 %copy-done.1 = f32[3,256]{1,0:T(4,128)} copy-done((f32[3,256]{1,0:T(4,128)}, f32[3,256]{1,0:T(4,128)S(1)}, u32[]{:S(2)}) %copy-start.1) | copy-done | bytes 3096
  22.5 0.0 copy-start.2
  22.5 0.6 %copy-done.2 = f32[3,256]{1,0:T(4,128)} copy-done((f32[3,256]{1,0:T(4,128)}, f32[3,256]{1,0:T(4,128)S(1)}, u32[]{:S(2)}) %copy-start.2) | copy-done | bytes 3096
  23.1 0.0 copy-start.3
  23.1 0.6 %copy-done.3 = f32[3,256]{1,0:T(4,128)} copy-done((f32[3,256]{1,0:T(4,128)}, f32[3,256]{1,0:T(4,128)S(1)}, u32[]{:S(2)}) %copy-start.3) | copy-done | bytes 3096
  23.7 0.0 copy-start.4
  23.7 0.6 %copy-done.4 = f32[3,256]{1,0:T(4,128)} copy-done((f32[3,256]{1,0:T(4,128)}, f32[3,256]{1,0:T(4,128)S(1)}, u32[]{:S(2)}) %copy-start.4) | copy-done | bytes 3096
  24.3 1.4 %shard_map.120 = (f32[3,256]{1,0:T(4,128)}, f32[3,256]{1,0:T(4,128)}, f32[3,256]{1,0:T(4,128)}, f32[3,256]{1,0:T(4,128)}, f32[6,2,24]{2,1,0:T(2,128)}) custom-call(f32[3,256]{1,0:T(4,128)} %copy-done.1, f32[3,256]{1,0:T(4,128)} %copy-done.2, f32[3,256]{1,0:T(4,128)} %copy-done.3, f32[3,256]{1,0:T(4,128)} %copy-done.4, f32[6,2,24]{2,1,0:T(2,128)} %copy-done), custom_call_target="tpu_custom_call" | custom-call | tf_op jit(solution)/shard_map/pallas_call | solution.py:323
Async XLA Ops:
  21.3 0.6 %copy-start = (f32[6,2,24]{2,1,0:T(2,128)}, f32[6,2,24]{2,1,0:T(2,128)S(1)}, u32[]{:S(2)}) copy-start(f32[6,2,24]{2,1,0:T(2,128)S(1)} %get-tuple-element.19.refs_4_) | copy-start | bytes 3460
  21.9 0.6 %copy-start.1 = (f32[3,256]{1,0:T(4,128)}, f32[3,256]{1,0:T(4,128)S(1)}, u32[]{:S(2)}) copy-start(f32[3,256]{1,0:T(4,128)S(1)} %get-tuple-element.15.refs_0_) | copy-start | bytes 9220
  22.5 0.6 %copy-start.2 = (f32[3,256]{1,0:T(4,128)}, f32[3,256]{1,0:T(4,128)S(1)}, u32[]{:S(2)}) copy-start(f32[3,256]{1,0:T(4,128)S(1)} %get-tuple-element.16.refs_1_) | copy-start | bytes 9220
  23.1 0.6 %copy-start.3 = (f32[3,256]{1,0:T(4,128)}, f32[3,256]{1,0:T(4,128)S(1)}, u32[]{:S(2)}) copy-start(f32[3,256]{1,0:T(4,128)S(1)} %get-tuple-element.17.refs_2_) | copy-start | bytes 9220
  23.7 0.6 %copy-start.4 = (f32[3,256]{1,0:T(4,128)}, f32[3,256]{1,0:T(4,128)S(1)}, u32[]{:S(2)}) copy-start(f32[3,256]{1,0:T(4,128)S(1)} %get-tuple-element.18.refs_3_) | copy-start | bytes 9220

commit v3 on v2

--- a/solution.py
+++ b/solution.py
@@ -65,9 +65,17 @@
     width = 1 << (act - 1).bit_length()
     group = math.gcd(LANES // width, chips)
 
-    def chip_at(k):
-        there = lax.rem(chip + k, chips)
-        return (there // per_blk, 2 * lax.rem(there, per_blk) + core)
+    def device_at(there, which_core):
+        return (there // per_blk, 2 * lax.rem(there, per_blk) + which_core)
+
+    def far_first(visit):
+        def turn(j, carry):
+            step = ((j + 1) // 2) * (1 - 2 * lax.rem(j, 2))
+            there = lax.rem(3 * chips - 1 + step - chip, chips)
+            visit(there, lax.rem(there - chip + chips, chips))
+            return carry
+
+        lax.fori_loop(0, chips, turn, 0)
 
     loads = [
         pltpu.make_async_copy(h, v, load_sem.at[i])
@@ -79,25 +87,42 @@
 
     barrier = pltpu.get_barrier_semaphore()
 
-    def greet(k, carry):
-        pl.semaphore_signal(barrier, inc=1, device_id=chip_at(k), device_id_type=MESH)
-        return carry
-
-    lax.fori_loop(1, chips, greet, 0)
-    pl.semaphore_signal(barrier, inc=1, device_id=partner, device_id_type=MESH)
+    def greet(there, k):
+        def signal(which_core):
+            pl.semaphore_signal(barrier, inc=1, device_id=device_at(there, which_core), device_id_type=MESH)
+
+        pl.when(k != 0)(lambda: signal(core))
+        signal(1 - core)
+
+    far_first(greet)
     for load in loads:
         load.start()
 
     def send_bulk(buffer, which):
-        def send(k, carry):
-            pltpu.make_async_remote_copy(
-                src_ref=buffer.at[0], dst_ref=buffer.at[k],
-                send_sem=bulk_send.at[which], recv_sem=bulk_recv.at[which, k // group],
-                device_id=chip_at(k), device_id_type=MESH,
-            ).start()
-            return carry
-
-        lax.fori_loop(1, chips, send, 0)
+        def send(there, k):
+            @pl.when(k != 0)
+            def _():
+                pltpu.make_async_remote_copy(
+                    src_ref=buffer.at[0], dst_ref=buffer.at[k],
+                    send_sem=bulk_send.at[which], recv_sem=bulk_recv.at[which, k // group],
+                    device_id=device_at(there, core), device_id_type=MESH,
+                ).start()
+
+        far_first(send)
+
+    def send_extra():
+        def send(there, k):
+            def copy(slot, which_core):
+                pltpu.make_async_remote_copy(
+                    src_ref=extra.at[0], dst_ref=extra.at[slot],
+                    send_sem=bulk_send.at[2], recv_sem=bulk_recv.at[2, 0],
+                    device_id=device_at(there, which_core), device_id_type=MESH,
+                ).start()
+
+            pl.when(k != 0)(lambda: copy(k, core))
+            copy(chips + k, 1 - core)
+
+        far_first(send)
 
     def arrival(buffer, which, first, count, sems):
         others = buffer.at[pl.ds(first, count)]
@@ -184,16 +209,30 @@
 
         return lax.fori_loop(1, chips // group, some, some(0, total))
 
-    def over_extra(targets, total, which=None):
-        def chunk(g, total):
-            if which is not None:
-                await_group(extra, which, g)
-            tile = extra[g * group]
-            for i in range(1, group):
-                tile = tile + extra[g * group + i]
-            return add_pairs(targets, [tile[c : c + 1] for c in range(7)], total)
-
-        return lax.fori_loop(1, chips // group, chunk, chunk(0, total))
+    blocks = LANES // width
+    block = lax.broadcasted_iota(jnp.int32, (2, LANES), 1) // width
+    first_block = [lax.rem(chip - i + 4 * chips, group) for i in range(group)]
+    masks = [[block == lax.rem(q + first_block[i], blocks) for i in range(group)] for q in range(4)]
+
+    def over_extra(targets, total):
+        groups = 2 * chips // group
+        batch = math.gcd(4, groups)
+
+        def some(b, total):
+            for g in range(batch):
+                slots = [extra[(b * batch + g) * group + i] for i in range(group)]
+                rows = [None] * 8
+                for q in range(4):
+                    both = jnp.where(masks[q][0], slots[0], 0.0)
+                    for i in range(1, group):
+                        both = jnp.where(masks[q][i], slots[i], both)
+                    if q > 0:
+                        both = pltpu.roll(both, LANES - q * width, 1)
+                    rows[q], rows[q + 4] = both[0:1], both[1:2]
+                total = add_pairs(targets, rows, total)
+            return total
+
+        return lax.fori_loop(0, groups // batch, some, total)
 
     def reduced(total):
         return packed([jnp.sum(part, axis=1, keepdims=True) for part in total])
@@ -209,7 +248,17 @@
     src2[0, 6:7, :] = jnp.where(hit_one, 0.0, mass)
     src2[0, 7:8, :] = jnp.zeros_like(mass)
     picker_two = picker_of(place_two, list_two)
-    pl.semaphore_wait(barrier, chips)
+    window = lane == sub_row + lax.rem(chip, group) * width
+
+    def in_slots(column):
+        return jnp.sum(jnp.where(window, column, 0.0), axis=0, keepdims=True)
+
+    slot_state = [
+        [in_slots(picked(picker_one, rows[c : c + 1])) for c in range(3)]
+        for rows in (pos, vel, acc, jerk)
+    ]
+    slot_mass = in_slots(picked(picker_one, mass))
+    pl.semaphore_wait(barrier, 2 * chips - 1)
     to_pair_one = pair_copy(tgt1, 0)
     to_pair_one.start()
     send_bulk(src1, 0)
@@ -221,39 +270,51 @@
     sums_one.start()
     sums_one.wait_recv()
     force_one = part1[0] + part1[1]
+
+    rows = spread(window, force_one)
+    moved = [None] * 8
+    for c in range(3):
+        state = correct(
+            slot_state[0][c], slot_state[1][c], slot_state[2][c], slot_state[3][c],
+            rows[c], rows[c + 3], STEP_BASE, True,
+        )
+        moved[c], moved[c + 3] = predict(*state, STEP_BASE)
+    moved[6], moved[7] = slot_mass, jnp.zeros_like(slot_mass)
+    for r in range(2):
+        line = moved[4 * r]
+        for q in range(1, 4):
+            line = line + pltpu.roll(jnp.broadcast_to(moved[4 * r + q], (8, LANES)), q * width, 1)[0:1]
+        extra[0, r : r + 1, :] = line
+    send_extra()
+
     rows = spread(picker_one, force_one)
     new_acc, new_jerk = jnp.concatenate(rows[0:3], axis=0), jnp.concatenate(rows[3:6], axis=0)
     pos, vel, acc, jerk = correct(pos, vel, acc, jerk, new_acc, new_jerk, stride, hit_one)
 
     elapsed = jnp.where(hit_one, STEP_BASE, 2 * STEP_BASE)
     pred_pos, pred_vel = predict(pos, vel, acc, jerk, elapsed)
-    columns = (
+    tgt2[0] = packed(
         [picked(picker_two, pred_pos[c : c + 1]) for c in range(3)]
         + [picked(picker_two, pred_vel[c : c + 1]) for c in range(3)]
-        + [picked(picker_two, jnp.where(hit_one, mass, 0.0))]
-    )
-    offset = lax.rem(chip, group) * width
-    window = lane == sub_row + offset
-    for c, column in enumerate(columns):
-        extra[0, c : c + 1, :] = jnp.sum(jnp.where(window, column, 0.0), axis=0, keepdims=True)
-    extra[0, 7:8, :] = jnp.zeros((1, LANES), jnp.float32)
-    send_bulk(extra, 2)
-    tgt2[0] = packed(columns[0:6])
+    )
     to_pair_two = pair_copy(tgt2, 2)
     to_pair_two.start()
     for c, row in enumerate(spread(place_one, force_one)):
         fresh_o[c, 0:1, :] = row[:, 0:act]
-
-    own_total = over_bulk([jnp.broadcast_to(c, (act, LANES)) for c in columns[0:6]], src2, zeros(), 1)
-    part2[2] = reduced(own_total)
+    own_targets = targets_of(tgt2[0])
+    own_total = over_bulk(own_targets, src2, zeros(), 1)
     to_pair_two.wait_recv()
-    targets = targets_of(tgt2[1])
-    total = over_bulk(targets, src2, zeros())
-    part2[0] = reduced(over_extra(targets, total, 2))
+    part2[0] = reduced(over_bulk(targets_of(tgt2[1]), src2, zeros()))
     sums_two = pair_copy(part2, 3)
     sums_two.start()
-    own_extra = reduced(over_extra(targets_of(tgt2[0]), zeros()))
-    own = part2[2] + own_extra
+    others = extra.at[pl.ds(1, 2 * chips - 1)]
+    all_extra = pltpu.make_async_remote_copy(
+        src_ref=others, dst_ref=others,
+        send_sem=bulk_send.at[2], recv_sem=bulk_recv.at[2, 0],
+        device_id=partner, device_id_type=MESH,
+    )
+    all_extra.wait_recv()
+    own = reduced(over_extra(own_targets, own_total))
     sums_two.wait_recv()
     force_two = own + part2[1]
     rows = spread(picker_two, force_two)
@@ -266,7 +327,8 @@
     for c, row in enumerate(spread(place_two, force_two)):
         fresh_o[c, 1:2, :] = row[:, 0:act]
 
-    for which, buffer in enumerate((src1, src2, extra)):
+    all_extra.wait_send()
+    for which, buffer in enumerate((src1, src2)):
         arrival(buffer, which, 1, chips - 1, 0).wait_send()
     for copy in (to_pair_one, sums_one, to_pair_two, sums_two):
         copy.wait_send()
@@ -302,11 +364,11 @@
             vmem((1, 2), jnp.int32),
             vmem((chips, 8, part_dev), jnp.float32),
             vmem((chips, 8, part_dev), jnp.float32),
-            vmem((chips, 8, LANES), jnp.float32),
+            vmem((2 * chips, 2, LANES), jnp.float32),
             vmem((2, act, LANES), jnp.float32),
             vmem((2, act, LANES), jnp.float32),
             vmem((2, act, LANES), jnp.float32),
-            vmem((3, act, LANES), jnp.float32),
+            vmem((2, act, LANES), jnp.float32),
             pltpu.SemaphoreType.DMA((8,)),
             pltpu.SemaphoreType.DMA((3,)),
             pltpu.SemaphoreType.DMA((3, chips)),
@@ -326,7 +388,8 @@
         in_specs=[pl.BlockSpec(memory_space=vmem)] * 5,
         out_specs=[pl.BlockSpec(memory_space=pltpu.HBM)] * 5,
         scratch_shapes=[pltpu.SemaphoreType.DMA((5,))],
-    )(*results)
+        compiler_params=pltpu.CompilerParams(vmem_limit_bytes=1024 * 1024),
+    )(*[pltpu.with_memory_space_constraint(value, vmem) for value in results])
     return (*written[0:4], written[4].transpose(1, 0, 2))
 
 

time: 25.9 us -> 21.4 us (0.83)
  local copies, waits for them, and re-layouts: 2.95 us -> 0 us
  Pallas kernels: 22.1 us -> 20.5 us
    unnamed x10 -> x0, local copies, waits for them, and re-layouts: 2.95 us -> none
    pallas_call x1, Pallas kernels: 20.7 us -> 19.9 us  [body(): pl.pallas_call(functools.partial(kernel, n_blk, n_grp, act), out_shape=(s...]
    pallas_call x1, Pallas kernels: 1.36 us -> 0.66 us  [body(): pl.pallas_call(write_out, out_shape=[jax.ShapeDtypeStruct(r.shape, r.dtyp...]
where the time goes in v3:
time: 21.4 us; the launch traced here: 21.2 us
  Pallas kernels  20.5 us (96%)
  between operations  0.64 us (3%)
    pallas_call x1, Pallas kernels, body(): pl.pallas_call(functools.partial(kernel, n_blk, n_grp, act), out_shape=(s...  19.9 us
    pallas_call x1, Pallas kernels, body(): pl.pallas_call(write_out, out_shape=[jax.ShapeDtypeStruct(r.shape, r.dtyp...  0.66 us

profile of v3, /device:TPU:0, one launch (start us, length us, event | category | flops | bytes accessed | tf_op | source)
XLA Modules:
  0.0 21.2 jit_solution(17555863394039892680)
XLA Ops:
  0.6 19.9 %shard_map.119 = (f32[3,256]{1,0:T(4,128)S(1)}, f32[3,256]{1,0:T(4,128)S(1)}, f32[3,256]{1,0:T(4,128)S(1)}, f32[3,256]{1,0:T(4,128)S(1)}, f32[6,2,24]{2,1,0:T(2,128)S(1)}) custom-call(f32[3,256]{1,0:T(4,128)} %pos_h.1, f32[3,256]{1,0:T(4,128)} %vel_h.1, f32[3,256]{1,0:T(4,128)} %acc_h.1, f32[3,256]{1,0:T(4,128)} %jerk_h.1, f32[1,256]{1,0:T(1,128)} %bitcast.4, ...), custom_call_target="tpu_custom_call" | custom-call | tf_op jit(solution)/shard_map/pallas_call | solution.py:351
  20.5 0.7 %shard_map.120 = (f32[3,256]{1,0:T(4,128)}, f32[3,256]{1,0:T(4,128)}, f32[3,256]{1,0:T(4,128)}, f32[3,256]{1,0:T(4,128)}, f32[6,2,24]{2,1,0:T(2,128)}) custom-call(f32[3,256]{1,0:T(4,128)S(1)} %get-tuple-element.15.refs_0_, f32[3,256]{1,0:T(4,128)S(1)} %get-tuple-element.16.refs_1_, f32[3,256]{1,0:T(4,128)S(1)} %get-tuple-element.17.refs_2_, ...), custom_call_target="tpu_custom_call" | custom-call | tf_op jit(solution)/shard_map/pallas_call | solution.py:385

commit v4 on v3

--- a/solution.py
+++ b/solution.py
@@ -112,15 +112,15 @@
 
     def send_extra():
         def send(there, k):
-            def copy(slot, which_core):
+            def copy(half, which_core):
                 pltpu.make_async_remote_copy(
-                    src_ref=extra.at[0], dst_ref=extra.at[slot],
-                    send_sem=bulk_send.at[2], recv_sem=bulk_recv.at[2, 0],
+                    src_ref=extra.at[0], dst_ref=extra.at[half * chips + k],
+                    send_sem=bulk_send.at[2], recv_sem=bulk_recv.at[2 + half, k // group],
                     device_id=device_at(there, which_core), device_id_type=MESH,
                 ).start()
 
-            pl.when(k != 0)(lambda: copy(k, core))
-            copy(chips + k, 1 - core)
+            pl.when(k != 0)(lambda: copy(0, core))
+            copy(1, 1 - core)
 
         far_first(send)
 
@@ -184,11 +184,11 @@
             tile = jnp.where(lane == c, column, tile)
         return tile
 
+    def spread_columns(mask, columns):
+        return [jnp.sum(jnp.where(mask, column, 0.0), axis=0, keepdims=True) for column in columns]
+
     def spread(mask, tile):
-        return [
-            jnp.sum(jnp.where(mask, tile[:, c : c + 1], 0.0), axis=0, keepdims=True)
-            for c in range(6)
-        ]
+        return spread_columns(mask, [tile[:, c : c + 1] for c in range(6)])
 
     def targets_of(tile):
         return [jnp.broadcast_to(tile[:, c : c + 1], (act, LANES)) for c in range(6)]
@@ -214,28 +214,42 @@
     first_block = [lax.rem(chip - i + 4 * chips, group) for i in range(group)]
     masks = [[block == lax.rem(q + first_block[i], blocks) for i in range(group)] for q in range(4)]
 
+    def extra_arrival(first, count, half, g):
+        others = extra.at[pl.ds(first, count)]
+        return pltpu.make_async_remote_copy(
+            src_ref=others, dst_ref=others,
+            send_sem=bulk_send.at[2], recv_sem=bulk_recv.at[2 + half, g],
+            device_id=partner, device_id_type=MESH,
+        )
+
     def over_extra(targets, total):
-        groups = 2 * chips // group
-        batch = math.gcd(4, groups)
-
-        def some(b, total):
-            for g in range(batch):
-                slots = [extra[(b * batch + g) * group + i] for i in range(group)]
-                rows = [None] * 8
-                for q in range(4):
-                    both = jnp.where(masks[q][0], slots[0], 0.0)
-                    for i in range(1, group):
-                        both = jnp.where(masks[q][i], slots[i], both)
-                    if q > 0:
-                        both = pltpu.roll(both, LANES - q * width, 1)
-                    rows[q], rows[q + 4] = both[0:1], both[1:2]
-                total = add_pairs(targets, rows, total)
-            return total
-
-        return lax.fori_loop(0, groups // batch, some, total)
+        groups = chips // group
+
+        def some(g, total):
+            if isinstance(g, int):
+                if group > 1:
+                    extra_arrival(1, group - 1, 0, g).wait_recv()
+            else:
+                extra_arrival(g * group, group, 0, g).wait_recv()
+            extra_arrival(chips + g * group, group, 1, g).wait_recv()
+            slots = [extra[g * group + i] + extra[chips + g * group + i] for i in range(group)]
+            rows = [None] * 8
+            for q in range(4):
+                both = jnp.where(masks[q][0], slots[0], 0.0)
+                for i in range(1, group):
+                    both = jnp.where(masks[q][i], slots[i], both)
+                if q > 0:
+                    both = pltpu.roll(both, LANES - q * width, 1)
+                rows[q], rows[q + 4] = both[0:1], both[1:2]
+            return add_pairs(targets, rows, total)
+
+        return some(0, lax.fori_loop(1, groups, lambda i, t: some(groups - i, t), total))
+
+    def columns_of(total):
+        return [jnp.sum(part, axis=1, keepdims=True) for part in total]
 
     def reduced(total):
-        return packed([jnp.sum(part, axis=1, keepdims=True) for part in total])
+        return packed(columns_of(total))
 
     picker_one = picker_of(place_one, list_one)
     tgt1[0] = packed(
@@ -265,13 +279,12 @@
     send_bulk(src2, 1)
     to_pair_one.wait_recv()
     targets = targets_of(tgt1[0] + tgt1[1])
-    part1[0] = reduced(over_bulk(targets, src1, zeros(), 0))
+    partial = columns_of(over_bulk(targets, src1, zeros(), 0))
+    part1[0] = packed(partial)
     sums_one = pair_copy(part1, 1)
     sums_one.start()
-    sums_one.wait_recv()
-    force_one = part1[0] + part1[1]
-
-    rows = spread(window, force_one)
+
+    rows = spread_columns(window, partial)
     moved = [None] * 8
     for c in range(3):
         state = correct(
@@ -287,6 +300,8 @@
         extra[0, r : r + 1, :] = line
     send_extra()
 
+    sums_one.wait_recv()
+    force_one = part1[0] + part1[1]
     rows = spread(picker_one, force_one)
     new_acc, new_jerk = jnp.concatenate(rows[0:3], axis=0), jnp.concatenate(rows[3:6], axis=0)
     pos, vel, acc, jerk = correct(pos, vel, acc, jerk, new_acc, new_jerk, stride, hit_one)
@@ -307,13 +322,6 @@
     part2[0] = reduced(over_bulk(targets_of(tgt2[1]), src2, zeros()))
     sums_two = pair_copy(part2, 3)
     sums_two.start()
-    others = extra.at[pl.ds(1, 2 * chips - 1)]
-    all_extra = pltpu.make_async_remote_copy(
-        src_ref=others, dst_ref=others,
-        send_sem=bulk_send.at[2], recv_sem=bulk_recv.at[2, 0],
-        device_id=partner, device_id_type=MESH,
-    )
-    all_extra.wait_recv()
     own = reduced(over_extra(own_targets, own_total))
     sums_two.wait_recv()
     force_two = own + part2[1]
@@ -327,7 +335,7 @@
     for c, row in enumerate(spread(place_two, force_two)):
         fresh_o[c, 1:2, :] = row[:, 0:act]
 
-    all_extra.wait_send()
+    extra_arrival(1, 2 * chips - 1, 0, 0).wait_send()
     for which, buffer in enumerate((src1, src2)):
         arrival(buffer, which, 1, chips - 1, 0).wait_send()
     for copy in (to_pair_one, sums_one, to_pair_two, sums_two):
@@ -371,7 +379,7 @@
             vmem((2, act, LANES), jnp.float32),
             pltpu.SemaphoreType.DMA((8,)),
             pltpu.SemaphoreType.DMA((3,)),
-            pltpu.SemaphoreType.DMA((3, chips)),
+            pltpu.SemaphoreType.DMA((4, chips)),
             pltpu.SemaphoreType.DMA((4,)),
             pltpu.SemaphoreType.DMA((4,)),
         ],

time: 21.4 us -> 20.8 us (0.972)
  Pallas kernels: 20.5 us -> 20 us
    pallas_call x1, Pallas kernels: 19.9 us -> 19.3 us  [body(): pl.pallas_call(functools.partial(kernel, n_blk, n_grp, act), out_shape=(s...]
where the time goes in v4:
time: 20.8 us; the launch traced here: 20.6 us
  Pallas kernels  20 us (96%)
  between operations  0.64 us (3%)
    pallas_call x1, Pallas kernels, body(): pl.pallas_call(functools.partial(kernel, n_blk, n_grp, act), out_shape=(s...  19.3 us
    pallas_call x1, Pallas kernels, body(): pl.pallas_call(write_out, out_shape=[jax.ShapeDtypeStruct(r.shape, r.dtyp...  0.66 us

profile of v4, /device:TPU:0, one launch (start us, length us, event | category | flops | bytes accessed | tf_op | source)
XLA Modules:
  0.0 20.6 jit_solution(5268358883321032489)
XLA Ops:
  0.6 19.3 %shard_map.119 = (f32[3,256]{1,0:T(4,128)S(1)}, f32[3,256]{1,0:T(4,128)S(1)}, f32[3,256]{1,0:T(4,128)S(1)}, f32[3,256]{1,0:T(4,128)S(1)}, f32[6,2,24]{2,1,0:T(2,128)S(1)}) custom-call(f32[3,256]{1,0:T(4,128)} %pos_h.1, f32[3,256]{1,0:T(4,128)} %vel_h.1, f32[3,256]{1,0:T(4,128)} %acc_h.1, f32[3,256]{1,0:T(4,128)} %jerk_h.1, f32[1,256]{1,0:T(1,128)} %bitcast.4, ...), custom_call_target="tpu_custom_call" | custom-call | tf_op jit(solution)/shard_map/pallas_call | solution.py:359
  20.0 0.7 %shard_map.120 = (f32[3,256]{1,0:T(4,128)}, f32[3,256]{1,0:T(4,128)}, f32[3,256]{1,0:T(4,128)}, f32[3,256]{1,0:T(4,128)}, f32[6,2,24]{2,1,0:T(2,128)}) custom-call(f32[3,256]{1,0:T(4,128)S(1)} %get-tuple-element.15.refs_0_, f32[3,256]{1,0:T(4,128)S(1)} %get-tuple-element.16.refs_1_, f32[3,256]{1,0:T(4,128)S(1)} %get-tuple-element.17.refs_2_, ...), custom_call_target="tpu_custom_call" | custom-call | tf_op jit(solution)/shard_map/pallas_call | solution.py:393

commit v5 on v4

--- a/solution.py
+++ b/solution.py
@@ -156,8 +156,7 @@
     pred_pos, pred_vel = predict(pos, vel, acc, jerk, STEP_BASE)
     src1[0, 0:3, :] = pred_pos
     src1[0, 3:6, :] = pred_vel
-    src1[0, 6:7, :] = mass
-    src1[0, 7:8, :] = jnp.zeros_like(mass)
+    src1[0, 6:7, :] = jnp.where(hit_one, -mass, mass)
 
     sub_row = lax.broadcasted_iota(jnp.int32, (act, LANES), 0)
     lane = lax.broadcasted_iota(jnp.int32, (act, LANES), 1)
@@ -196,18 +195,23 @@
     def zeros():
         return tuple(jnp.zeros((act, LANES), jnp.float32) for _ in range(6))
 
-    def over_bulk(targets, buffer, total, which=None):
+    def over_bulk(targets, buffer, total, which=None, after_first=None):
         def some(g, total):
             if which is not None:
                 await_group(buffer, which, g)
             for i in range(group):
                 for start in range(0, part_dev, LANES):
                     k = g * group + i
-                    rows = [buffer[k, c : c + 1, start : start + LANES] for c in range(7)]
+                    rows = [buffer[k, c : c + 1, start : start + LANES] for c in range(6)]
+                    signed = src1[k, 6:7, start : start + LANES]
+                    rows.append(jnp.abs(signed) if buffer is src1 else jnp.maximum(signed, 0.0))
                     total = add_pairs(targets, rows, total)
             return total
 
-        return lax.fori_loop(1, chips // group, some, some(0, total))
+        total = some(0, total)
+        if after_first is not None:
+            after_first()
+        return lax.fori_loop(1, chips // group, some, total)
 
     blocks = LANES // width
     block = lax.broadcasted_iota(jnp.int32, (2, LANES), 1) // width
@@ -259,8 +263,6 @@
     late_pos, late_vel = predict(pos, vel, acc, jerk, 2 * STEP_BASE)
     src2[0, 0:3, :] = late_pos
     src2[0, 3:6, :] = late_vel
-    src2[0, 6:7, :] = jnp.where(hit_one, 0.0, mass)
-    src2[0, 7:8, :] = jnp.zeros_like(mass)
     picker_two = picker_of(place_two, list_two)
     window = lane == sub_row + lax.rem(chip, group) * width
 
@@ -276,10 +278,9 @@
     to_pair_one = pair_copy(tgt1, 0)
     to_pair_one.start()
     send_bulk(src1, 0)
-    send_bulk(src2, 1)
     to_pair_one.wait_recv()
     targets = targets_of(tgt1[0] + tgt1[1])
-    partial = columns_of(over_bulk(targets, src1, zeros(), 0))
+    partial = columns_of(over_bulk(targets, src1, zeros(), 0, lambda: send_bulk(src2, 1)))
     part1[0] = packed(partial)
     sums_one = pair_copy(part1, 1)
     sums_one.start()
@@ -370,8 +371,8 @@
             vmem((1, part_dev), jnp.int32),
             vmem((2, act), jnp.int32),
             vmem((1, 2), jnp.int32),
-            vmem((chips, 8, part_dev), jnp.float32),
-            vmem((chips, 8, part_dev), jnp.float32),
+            vmem((chips, 7, part_dev), jnp.float32),
+            vmem((chips, 6, part_dev), jnp.float32),
             vmem((2 * chips, 2, LANES), jnp.float32),
             vmem((2, act, LANES), jnp.float32),
             vmem((2, act, LANES), jnp.float32),

time: 20.8 us -> 20.5 us (0.986)
  Pallas kernels: 20 us -> 19.6 us
    pallas_call x1, Pallas kernels: 19.3 us -> 18.9 us  [body(): pl.pallas_call(functools.partial(kernel, n_blk, n_grp, act), out_shape=(s...]
where the time goes in v5:
time: 20.5 us; the launch traced here: 20.2 us
  Pallas kernels  19.6 us (96%)
  between operations  0.64 us (3%)
    pallas_call x1, Pallas kernels, body(): pl.pallas_call(functools.partial(kernel, n_blk, n_grp, act), out_shape=(s...  18.9 us
    pallas_call x1, Pallas kernels, body(): pl.pallas_call(write_out, out_shape=[jax.ShapeDtypeStruct(r.shape, r.dtyp...  0.66 us

profile of v5, /device:TPU:0, one launch (start us, length us, event | category | flops | bytes accessed | tf_op | source)
XLA Modules:
  0.0 20.2 jit_solution(959889117068028087)
XLA Ops:
  0.6 18.9 %shard_map.119 = (f32[3,256]{1,0:T(4,128)S(1)}, f32[3,256]{1,0:T(4,128)S(1)}, f32[3,256]{1,0:T(4,128)S(1)}, f32[3,256]{1,0:T(4,128)S(1)}, f32[6,2,24]{2,1,0:T(2,128)S(1)}) custom-call(f32[3,256]{1,0:T(4,128)} %pos_h.1, f32[3,256]{1,0:T(4,128)} %vel_h.1, f32[3,256]{1,0:T(4,128)} %acc_h.1, f32[3,256]{1,0:T(4,128)} %jerk_h.1, f32[1,256]{1,0:T(1,128)} %bitcast.4, ...), custom_call_target="tpu_custom_call" | custom-call | tf_op jit(solution)/shard_map/pallas_call | solution.py:360
  19.6 0.7 %shard_map.120 = (f32[3,256]{1,0:T(4,128)}, f32[3,256]{1,0:T(4,128)}, f32[3,256]{1,0:T(4,128)}, f32[3,256]{1,0:T(4,128)}, f32[6,2,24]{2,1,0:T(2,128)}) custom-call(f32[3,256]{1,0:T(4,128)S(1)} %get-tuple-element.15.refs_0_, f32[3,256]{1,0:T(4,128)S(1)} %get-tuple-element.16.refs_1_, f32[3,256]{1,0:T(4,128)S(1)} %get-tuple-element.17.refs_2_, ...), custom_call_target="tpu_custom_call" | custom-call | tf_op jit(solution)/shard_map/pallas_call | solution.py:394

commit v6 on v5

--- a/solution.py
+++ b/solution.py
@@ -195,7 +195,7 @@
     def zeros():
         return tuple(jnp.zeros((act, LANES), jnp.float32) for _ in range(6))
 
-    def over_bulk(targets, buffer, total, which=None, after_first=None):
+    def over_bulk(targets, buffer, total, which=None):
         def some(g, total):
             if which is not None:
                 await_group(buffer, which, g)
@@ -208,10 +208,7 @@
                     total = add_pairs(targets, rows, total)
             return total
 
-        total = some(0, total)
-        if after_first is not None:
-            after_first()
-        return lax.fori_loop(1, chips // group, some, total)
+        return lax.fori_loop(1, chips // group, some, some(0, total))
 
     blocks = LANES // width
     block = lax.broadcasted_iota(jnp.int32, (2, LANES), 1) // width
@@ -279,8 +276,9 @@
     to_pair_one.start()
     send_bulk(src1, 0)
     to_pair_one.wait_recv()
+    send_bulk(src2, 1)
     targets = targets_of(tgt1[0] + tgt1[1])
-    partial = columns_of(over_bulk(targets, src1, zeros(), 0, lambda: send_bulk(src2, 1)))
+    partial = columns_of(over_bulk(targets, src1, zeros(), 0))
     part1[0] = packed(partial)
     sums_one = pair_copy(part1, 1)
     sums_one.start()

time: 20.5 us -> 20.8 us (1.015)
  Pallas kernels: 19.6 us -> 20 us
    pallas_call x1, Pallas kernels: 18.9 us -> 19.3 us  [body(): pl.pallas_call(functools.partial(kernel, n_blk, n_grp, act), out_shape=(s...]
where the time goes in v6:
time: 20.8 us; the launch traced here: 20.6 us
  Pallas kernels  20 us (96%)
  between operations  0.64 us (3%)
    pallas_call x1, Pallas kernels, body(): pl.pallas_call(functools.partial(kernel, n_blk, n_grp, act), out_shape=(s...  19.3 us
    pallas_call x1, Pallas kernels, body(): pl.pallas_call(write_out, out_shape=[jax.ShapeDtypeStruct(r.shape, r.dtyp...  0.66 us

profile of v6, /device:TPU:0, one launch (start us, length us, event | category | flops | bytes accessed | tf_op | source)
XLA Modules:
  0.0 20.6 jit_solution(13411474729418245718)
XLA Ops:
  0.6 19.3 %shard_map.119 = (f32[3,256]{1,0:T(4,128)S(1)}, f32[3,256]{1,0:T(4,128)S(1)}, f32[3,256]{1,0:T(4,128)S(1)}, f32[3,256]{1,0:T(4,128)S(1)}, f32[6,2,24]{2,1,0:T(2,128)S(1)}) custom-call(f32[3,256]{1,0:T(4,128)} %pos_h.1, f32[3,256]{1,0:T(4,128)} %vel_h.1, f32[3,256]{1,0:T(4,128)} %acc_h.1, f32[3,256]{1,0:T(4,128)} %jerk_h.1, f32[1,256]{1,0:T(1,128)} %bitcast.4, ...), custom_call_target="tpu_custom_call" | custom-call | tf_op jit(solution)/shard_map/pallas_call | solution.py:358
  20.0 0.7 %shard_map.120 = (f32[3,256]{1,0:T(4,128)}, f32[3,256]{1,0:T(4,128)}, f32[3,256]{1,0:T(4,128)}, f32[3,256]{1,0:T(4,128)}, f32[6,2,24]{2,1,0:T(2,128)}) custom-call(f32[3,256]{1,0:T(4,128)S(1)} %get-tuple-element.15.refs_0_, f32[3,256]{1,0:T(4,128)S(1)} %get-tuple-element.16.refs_1_, f32[3,256]{1,0:T(4,128)S(1)} %get-tuple-element.17.refs_2_, ...), custom_call_target="tpu_custom_call" | custom-call | tf_op jit(solution)/shard_map/pallas_call | solution.py:392

commit v7 on v6

--- a/solution.py
+++ b/solution.py
@@ -257,6 +257,11 @@
         [picked(picker_one, pred_pos[c : c + 1]) for c in range(3)]
         + [picked(picker_one, pred_vel[c : c + 1]) for c in range(3)]
     )
+    pl.semaphore_wait(barrier, 2 * chips - 1)
+    to_pair_one = pair_copy(tgt1, 0)
+    to_pair_one.start()
+    send_bulk(src1, 0)
+    to_pair_one.wait_recv()
     late_pos, late_vel = predict(pos, vel, acc, jerk, 2 * STEP_BASE)
     src2[0, 0:3, :] = late_pos
     src2[0, 3:6, :] = late_vel
@@ -271,11 +276,6 @@
         for rows in (pos, vel, acc, jerk)
     ]
     slot_mass = in_slots(picked(picker_one, mass))
-    pl.semaphore_wait(barrier, 2 * chips - 1)
-    to_pair_one = pair_copy(tgt1, 0)
-    to_pair_one.start()
-    send_bulk(src1, 0)
-    to_pair_one.wait_recv()
     send_bulk(src2, 1)
     targets = targets_of(tgt1[0] + tgt1[1])
     partial = columns_of(over_bulk(targets, src1, zeros(), 0))

time: 20.8 us -> 20.8 us (level)
  no operation moved by 1% of the time
where the time goes in v7:
time: 20.8 us; the launch traced here: 20.6 us
  Pallas kernels  20 us (96%)
  between operations  0.64 us (3%)
    pallas_call x1, Pallas kernels, body(): pl.pallas_call(functools.partial(kernel, n_blk, n_grp, act), out_shape=(s...  19.3 us
    pallas_call x1, Pallas kernels, body(): pl.pallas_call(write_out, out_shape=[jax.ShapeDtypeStruct(r.shape, r.dtyp...  0.66 us

profile of v7, /device:TPU:0, one launch (start us, length us, event | category | flops | bytes accessed | tf_op | source)
XLA Modules:
  0.0 20.6 jit_solution(10023465863636206666)
XLA Ops:
  0.6 19.3 %shard_map.119 = (f32[3,256]{1,0:T(4,128)S(1)}, f32[3,256]{1,0:T(4,128)S(1)}, f32[3,256]{1,0:T(4,128)S(1)}, f32[3,256]{1,0:T(4,128)S(1)}, f32[6,2,24]{2,1,0:T(2,128)S(1)}) custom-call(f32[3,256]{1,0:T(4,128)} %pos_h.1, f32[3,256]{1,0:T(4,128)} %vel_h.1, f32[3,256]{1,0:T(4,128)} %acc_h.1, f32[3,256]{1,0:T(4,128)} %jerk_h.1, f32[1,256]{1,0:T(1,128)} %bitcast.4, ...), custom_call_target="tpu_custom_call" | custom-call | tf_op jit(solution)/shard_map/pallas_call | solution.py:358
  20.0 0.7 %shard_map.120 = (f32[3,256]{1,0:T(4,128)}, f32[3,256]{1,0:T(4,128)}, f32[3,256]{1,0:T(4,128)}, f32[3,256]{1,0:T(4,128)}, f32[6,2,24]{2,1,0:T(2,128)}) custom-call(f32[3,256]{1,0:T(4,128)S(1)} %get-tuple-element.15.refs_0_, f32[3,256]{1,0:T(4,128)S(1)} %get-tuple-element.16.refs_1_, f32[3,256]{1,0:T(4,128)S(1)} %get-tuple-element.17.refs_2_, ...), custom_call_target="tpu_custom_call" | custom-call | tf_op jit(solution)/shard_map/pallas_call | solution.py:392

commit v8 on v7

--- a/solution.py
+++ b/solution.py
@@ -195,9 +195,9 @@
     def zeros():
         return tuple(jnp.zeros((act, LANES), jnp.float32) for _ in range(6))
 
-    def over_bulk(targets, buffer, total, which=None):
+    def over_bulk(targets, buffer, total, which=None, awaited=0):
         def some(g, total):
-            if which is not None:
+            if which is not None and not (isinstance(g, int) and g < awaited):
                 await_group(buffer, which, g)
             for i in range(group):
                 for start in range(0, part_dev, LANES):
@@ -276,9 +276,10 @@
         for rows in (pos, vel, acc, jerk)
     ]
     slot_mass = in_slots(picked(picker_one, mass))
+    await_group(src1, 0, 0)
     send_bulk(src2, 1)
     targets = targets_of(tgt1[0] + tgt1[1])
-    partial = columns_of(over_bulk(targets, src1, zeros(), 0))
+    partial = columns_of(over_bulk(targets, src1, zeros(), 0, 1))
     part1[0] = packed(partial)
     sums_one = pair_copy(part1, 1)
     sums_one.start()

time: 20.8 us -> 20.3 us (0.976)
  Pallas kernels: 20 us -> 19.5 us
    pallas_call x1, Pallas kernels: 19.3 us -> 18.8 us  [body(): pl.pallas_call(functools.partial(kernel, n_blk, n_grp, act), out_shape=(s...]
where the time goes in v8:
time: 20.3 us; the launch traced here: 20.1 us
  Pallas kernels  19.5 us (96%)
  between operations  0.64 us (3%)
    pallas_call x1, Pallas kernels, body(): pl.pallas_call(functools.partial(kernel, n_blk, n_grp, act), out_shape=(s...  18.8 us
    pallas_call x1, Pallas kernels, body(): pl.pallas_call(write_out, out_shape=[jax.ShapeDtypeStruct(r.shape, r.dtyp...  0.66 us

profile of v8, /device:TPU:0, one launch (start us, length us, event | category | flops | bytes accessed | tf_op | source)
XLA Modules:
  0.0 20.1 jit_solution(15259277093027163358)
XLA Ops:
  0.6 18.8 %shard_map.119 = (f32[3,256]{1,0:T(4,128)S(1)}, f32[3,256]{1,0:T(4,128)S(1)}, f32[3,256]{1,0:T(4,128)S(1)}, f32[3,256]{1,0:T(4,128)S(1)}, f32[6,2,24]{2,1,0:T(2,128)S(1)}) custom-call(f32[3,256]{1,0:T(4,128)} %pos_h.1, f32[3,256]{1,0:T(4,128)} %vel_h.1, f32[3,256]{1,0:T(4,128)} %acc_h.1, f32[3,256]{1,0:T(4,128)} %jerk_h.1, f32[1,256]{1,0:T(1,128)} %bitcast.4, ...), custom_call_target="tpu_custom_call" | custom-call | tf_op jit(solution)/shard_map/pallas_call | solution.py:359
  19.5 0.7 %shard_map.120 = (f32[3,256]{1,0:T(4,128)}, f32[3,256]{1,0:T(4,128)}, f32[3,256]{1,0:T(4,128)}, f32[3,256]{1,0:T(4,128)}, f32[6,2,24]{2,1,0:T(2,128)}) custom-call(f32[3,256]{1,0:T(4,128)S(1)} %get-tuple-element.15.refs_0_, f32[3,256]{1,0:T(4,128)S(1)} %get-tuple-element.16.refs_1_, f32[3,256]{1,0:T(4,128)S(1)} %get-tuple-element.17.refs_2_, ...), custom_call_target="tpu_custom_call" | custom-call | tf_op jit(solution)/shard_map/pallas_call | solution.py:393

commit v9 on v8

--- a/solution.py
+++ b/solution.py
@@ -276,8 +276,10 @@
         for rows in (pos, vel, acc, jerk)
     ]
     slot_mass = in_slots(picked(picker_one, mass))
+    early = lax.rem(chip, per_blk) < per_blk // 4
+    pl.when(early)(lambda: send_bulk(src2, 1))
     await_group(src1, 0, 0)
-    send_bulk(src2, 1)
+    pl.when(jnp.logical_not(early))(lambda: send_bulk(src2, 1))
     targets = targets_of(tgt1[0] + tgt1[1])
     partial = columns_of(over_bulk(targets, src1, zeros(), 0, 1))
     part1[0] = packed(partial)

time: 20.3 us -> 20.8 us (1.025)
  Pallas kernels: 19.5 us -> 20 us
    pallas_call x1, Pallas kernels: 18.8 us -> 19.3 us  [body(): pl.pallas_call(functools.partial(kernel, n_blk, n_grp, act), out_shape=(s...]
where the time goes in v9:
time: 20.8 us; the launch traced here: 20.6 us
  Pallas kernels  20 us (96%)
  between operations  0.64 us (3%)
    pallas_call x1, Pallas kernels, body(): pl.pallas_call(functools.partial(kernel, n_blk, n_grp, act), out_shape=(s...  19.3 us
    pallas_call x1, Pallas kernels, body(): pl.pallas_call(write_out, out_shape=[jax.ShapeDtypeStruct(r.shape, r.dtyp...  0.66 us

profile of v9, /device:TPU:0, one launch (start us, length us, event | category | flops | bytes accessed | tf_op | source)
XLA Modules:
  0.0 20.6 jit_solution(12544804485406583818)
XLA Ops:
  0.6 19.3 %shard_map.119 = (f32[3,256]{1,0:T(4,128)S(1)}, f32[3,256]{1,0:T(4,128)S(1)}, f32[3,256]{1,0:T(4,128)S(1)}, f32[3,256]{1,0:T(4,128)S(1)}, f32[6,2,24]{2,1,0:T(2,128)S(1)}) custom-call(f32[3,256]{1,0:T(4,128)} %pos_h.1, f32[3,256]{1,0:T(4,128)} %vel_h.1, f32[3,256]{1,0:T(4,128)} %acc_h.1, f32[3,256]{1,0:T(4,128)} %jerk_h.1, f32[1,256]{1,0:T(1,128)} %bitcast.4, ...), custom_call_target="tpu_custom_call" | custom-call | tf_op jit(solution)/shard_map/pallas_call | solution.py:361
  19.9 0.7 %shard_map.120 = (f32[3,256]{1,0:T(4,128)}, f32[3,256]{1,0:T(4,128)}, f32[3,256]{1,0:T(4,128)}, f32[3,256]{1,0:T(4,128)}, f32[6,2,24]{2,1,0:T(2,128)}) custom-call(f32[3,256]{1,0:T(4,128)S(1)} %get-tuple-element.15.refs_0_, f32[3,256]{1,0:T(4,128)S(1)} %get-tuple-element.16.refs_1_, f32[3,256]{1,0:T(4,128)S(1)} %get-tuple-element.17.refs_2_, ...), custom_call_target="tpu_custom_call" | custom-call | tf_op jit(solution)/shard_map/pallas_call | solution.py:395
